TPU v7x, 256 devices: a whole 4x4x8 slice. The times are simulated.
256 devices in a mesh: dp: 8 (over y, x_lo), context: 8 (over z), tensor: 4 (over x_hi, core).
Axes of the slice: x: 4 (x_hi: 2, x_lo: 2; x = x_hi * 2 + x_lo), y: 4, z: 8, core: 2. Of those that a mesh axis runs over, the one named last changes fastest.
Arguments:
- layer_input: bfloat16 [8, 4096, 8192], P('dp', 'context'), may hold values from -60 to 60
- queries: bfloat16 [8, 4096, 4096], P('dp', 'context', 'tensor'), may hold values from -6 to 6
- rotated_key_states: bfloat16 [8, 4096, 512], P('dp', 'context', 'tensor'), may hold values from -6 to 6
- values: bfloat16 [8, 4096, 512], P('dp', 'context', 'tensor'), may hold values from -6 to 6
- attention_out: bfloat16 [8, 4096, 4096], P('dp', 'context', 'tensor'), may hold values from -6 to 6
- output_grad: bfloat16 [8, 4096, 4096], P('dp', 'context', 'tensor'), may hold values from -6 to 6
- normalizer_shift: float32 [32], P('tensor'), may hold values from 0 to 1.5
- document_lengths: int32 [8, 16], P('dp'), may hold values from 1 to 3072, 4096 in all within a row
- dither: int32 [2, 8192, 512], P(None, ('dp', 'context'), 'tensor'), may hold values from 0 to 255
Outputs:
- query_grad: bfloat16 [8, 4096, 4096], P('dp', 'context', 'tensor')
- weight_codes: float32 [2, 8192, 512], P(None, ('dp', 'context'), 'tensor')
Inputs may be any that keep to these rules, and one draw needn't show every extreme that they name: `document_lengths`: each sequence's lengths sum to 4096, and its longest document has exactly 3072 positions.
All inputs are finite; a program needn't handle non-finite values. Where the computation divides by a largest or mean magnitude, that divisor is 1e-20 or more.
Results may differ from a plain program's by a relative error of at most 0.0064.
Values may be sent and summed in bfloat16 or wider, within the bound.
No kernel may reach another device: no remote copies, remote signals or barrier semaphores. Data moves between devices by JAX's collectives and lax.ppermute only.
A program may use at most 64 MiB of HBM per device.

v0:
```python
import functools
import math

import jax
import jax.numpy as jnp
from jax import lax
from jax.experimental import pallas as pl
from jax.experimental.pallas import tpu as pltpu
from jax.sharding import PartitionSpec as P

HEAD_SIZE = 128
SOFTMAX_SCALE = HEAD_SIZE ** (-0.5)
LOG2_E = math.log2(math.e)
KEY_TILE = 256
HEADS_PER_STEP = 4
VMEM_LIMIT = 40 << 20
F32 = jnp.float32
BF16 = jnp.bfloat16

NT = (((1,), (1,)), ((), ()))
NN = (((1,), (0,)), ((), ()))
TN = (((0,), (0,)), ((), ()))


def dot(a, b, dims):
    return lax.dot_general(a, b, dims, preferred_element_type=F32)


def vmem_params():
    return pltpu.CompilerParams(vmem_limit_bytes=VMEM_LIMIT)


def opening_of(lengths_ref, position):
    total = jnp.int32(0)
    opening = jnp.zeros_like(position)
    for n in range(lengths_ref.shape[1]):
        total = total + lengths_ref[0, n]
        opening = jnp.where(total <= position, total, opening)
    return opening


def prepare_body(
    rank_ref,
    core_ref,
    lengths_ref,
    shift_ref,
    o_ref,
    do_ref,
    features_ref,
    delta_ref,
    norm_ref,
    opening_ref,
    bounds_ref,
    parts_ref,
    sem,
):
    count, _, half = parts_ref.shape
    copies = []
    for n in range(count):
        first = pl.multiple_of((2 * n + core_ref[0]) * half, half)
        copies.append(
            pltpu.make_async_copy(features_ref.at[:, pl.ds(first, half)], parts_ref.at[n], sem.at[n])
        )
        copies[n].start()
    heads, rows = delta_ref.shape[0], delta_ref.shape[2]
    start = rank_ref[0] * rows
    bounds_ref[0] = opening_of(lengths_ref, start)
    bounds_ref[1] = opening_of(lengths_ref, start + rows - 1)
    position = start + lax.broadcasted_iota(jnp.int32, opening_ref.shape, 1)
    opening = opening_of(lengths_ref, position)
    opening_ref[...] = opening
    log_visible = jnp.log((position - opening + 1).astype(F32))[0:1, :]
    for h in range(heads):
        lanes = slice(h * HEAD_SIZE, (h + 1) * HEAD_SIZE)
        product = o_ref[:, lanes].astype(F32) * do_ref[:, lanes].astype(F32)
        delta_ref[h] = jnp.sum(product.T, axis=0, keepdims=True)
        norm_ref[h] = (log_visible + shift_ref[h]) * LOG2_E
    for copy in copies:
        copy.wait()


def prepare(rank, core, lengths, head_shift, o, do, features, parts):
    rows, width = o.shape
    heads = width // HEAD_SIZE
    smem = pl.BlockSpec(memory_space=pltpu.SMEM)
    vmem = pl.BlockSpec(memory_space=pltpu.VMEM)
    return pl.pallas_call(
        prepare_body,
        in_specs=[smem, smem, smem, smem, vmem, vmem, pl.BlockSpec(memory_space=pltpu.HBM)],
        out_specs=[vmem, vmem, vmem, smem, pl.BlockSpec(memory_space=pltpu.HBM)],
        out_shape=[
            jax.ShapeDtypeStruct((heads, 1, rows), F32),
            jax.ShapeDtypeStruct((heads, 1, rows), F32),
            jax.ShapeDtypeStruct((8, rows), jnp.int32),
            jax.ShapeDtypeStruct((2,), jnp.int32),
            jax.ShapeDtypeStruct((parts, rows, features.shape[1] // parts // 2), BF16),
        ],
        scratch_shapes=[pltpu.SemaphoreType.DMA((parts,))],
        compiler_params=vmem_params(),
        name="prepare",
    )(rank, core, lengths, head_shift, o, do, features)


def attention_body(shifts, first, last, *refs):
    blocks = len(shifts)
    rank_ref, bounds_ref, q_ref, do_ref, delta_ref, norm_ref, opening_ref = refs[:7]
    rest = list(refs[7:])
    kv_refs = [rest.pop(0) for _ in range(blocks)]
    dq_in_ref = None if first else rest.pop(0)
    dq_ref = rest.pop(0)
    dkv_refs = [rest.pop(0) for _ in range(blocks)]
    acc_ref, key_t_ref, held_ref, dq_acc_ref = rest
    step = pl.program_id(0)
    rows = q_ref.shape[0]
    start = rank_ref[0] * rows
    first_opening, last_opening = bounds_ref[0], bounds_ref[1]

    @pl.when(step == 0)
    def _():
        acc_ref[...] = jnp.zeros_like(acc_ref)
        for b in range(blocks):
            held_ref[b] = kv_refs[b][...]
            key_t_ref[b] = kv_refs[b][:, :HEAD_SIZE].T

    dq_acc_ref[...] = jnp.zeros_like(dq_acc_ref) if first else dq_in_ref[...]

    def tile(b, key_start, heads, k0, q0, own, masked):
        k = held_ref[b, k0 : k0 + KEY_TILE, :HEAD_SIZE]
        v = held_ref[b, k0 : k0 + KEY_TILE, HEAD_SIZE:]
        if masked:
            shape = (KEY_TILE, rows - q0)
            key = (key_start + k0) + lax.broadcasted_iota(jnp.int32, shape, 0)
            allowed = key >= opening_ref[0:1, q0:]
            if own:
                query = (start + q0) + lax.broadcasted_iota(jnp.int32, shape, 1)
                allowed = allowed & (key <= query)
        for j in heads:
            lanes = pl.ds(j * HEAD_SIZE if isinstance(j, int) else pl.multiple_of(j * HEAD_SIZE, HEAD_SIZE), HEAD_SIZE)
            q = q_ref[q0:, lanes]
            do = do_ref[q0:, lanes]
            scores = dot(k, q, NT)
            probs = jnp.exp2(scores * (SOFTMAX_SCALE * LOG2_E) - norm_ref[j, :, q0:])
            if masked:
                probs = jnp.where(allowed, probs, 0.0)
            prob_grad = dot(v, do, NT)
            score_grad = (probs * (prob_grad - delta_ref[j, :, q0:])).astype(BF16)
            acc_ref[b, k0 : k0 + KEY_TILE, HEAD_SIZE:] += dot(probs.astype(BF16), do, NN)
            acc_ref[b, k0 : k0 + KEY_TILE, :HEAD_SIZE] += dot(score_grad, q, NN)
            dq_acc_ref[j, :, q0:] += dot(key_t_ref[b, :, k0 : k0 + KEY_TILE], score_grad, NN)

    def whole_block(b, key_start):
        for k0 in range(0, rows, KEY_TILE):
            tile(b, key_start, range(HEADS_PER_STEP), k0, 0, False, False)

    def masked_block(b, key_start, own):
        def pair(n, _):
            for k0 in range(0, rows, KEY_TILE):
                tile(b, key_start, (2 * n, 2 * n + 1), k0, k0 if own else 0, own, True)
            return 0

        lax.fori_loop(0, HEADS_PER_STEP // 2, pair, 0)

    def block(b, shift):
        key_start = start - shift * rows
        reached = (key_start >= 0) & (first_opening < key_start + rows)
        whole = last_opening <= key_start

        @pl.when(reached & whole)
        def _():
            whole_block(b, key_start)

        @pl.when(reached & jnp.logical_not(whole))
        def _():
            masked_block(b, key_start, False)

    if shifts == (0,):
        masked_block(0, start, True)
    elif blocks == 1:
        block(0, shifts[0])
    else:

        def each(b, _):
            block(b, jnp.where(b == 0, shifts[0], shifts[1]))
            return 0

        lax.fori_loop(0, blocks, each, 0)

    if last:
        for j in range(HEADS_PER_STEP):
            total = dq_acc_ref[j] * SOFTMAX_SCALE
            dq_ref[:, j * HEAD_SIZE : (j + 1) * HEAD_SIZE] = total.T.astype(BF16)
    else:
        dq_ref[...] = dq_acc_ref[...]

    @pl.when(step == pl.num_programs(0) - 1)
    def _():
        for b in range(blocks):
            dkv_refs[b][:, :HEAD_SIZE] = (acc_ref[b, :, :HEAD_SIZE] * SOFTMAX_SCALE).astype(dkv_refs[b].dtype)
            dkv_refs[b][:, HEAD_SIZE:] = acc_ref[b, :, HEAD_SIZE:].astype(dkv_refs[b].dtype)


def attention_step(shifts, first, last, rank, bounds, q, do, delta, norm, opening, kvs, dq):
    rows, width = q.shape
    heads = width // HEAD_SIZE
    blocks = len(shifts)
    smem = pl.BlockSpec(memory_space=pltpu.SMEM)
    head_block = pl.BlockSpec((rows, HEADS_PER_STEP * HEAD_SIZE), lambda h: (0, h))
    row_block = pl.BlockSpec((HEADS_PER_STEP, 1, rows), lambda h: (h, 0, 0))
    dq_block = pl.BlockSpec((HEADS_PER_STEP, HEAD_SIZE, rows), lambda h: (h, 0, 0))
    kv_block = pl.BlockSpec((rows, 2 * HEAD_SIZE), lambda h: (0, 0))
    opening_block = pl.BlockSpec(opening.shape, lambda h: (0, 0))
    in_specs = [smem, smem, head_block, head_block, row_block, row_block, opening_block]
    in_specs += [kv_block] * blocks + ([] if first else [dq_block])
    if last:
        out_specs = [head_block]
        out_shape = [jax.ShapeDtypeStruct((rows, width), BF16)]
    else:
        out_specs = [dq_block]
        out_shape = [jax.ShapeDtypeStruct((heads, HEAD_SIZE, rows), F32)]
    for s in shifts:
        out_specs.append(kv_block)
        out_shape.append(jax.ShapeDtypeStruct((rows, 2 * HEAD_SIZE), F32 if s == 0 else BF16))
    pairs = heads * rows * rows * blocks
    return pl.pallas_call(
        functools.partial(attention_body, shifts, first, last),
        grid=(heads // HEADS_PER_STEP,),
        in_specs=in_specs,
        out_specs=out_specs,
        out_shape=out_shape,
        scratch_shapes=[
            pltpu.VMEM((blocks, rows, 2 * HEAD_SIZE), F32),
            pltpu.VMEM((blocks, HEAD_SIZE, rows), BF16),
            pltpu.VMEM((blocks, rows, 2 * HEAD_SIZE), BF16),
            pltpu.VMEM((HEADS_PER_STEP, HEAD_SIZE, rows), F32),
        ],
        cost_estimate=pl.CostEstimate(flops=pairs, bytes_accessed=1 << 20, transcendentals=0),
        compiler_params=vmem_params(),
        name="attention_" + "_".join(str(s) for s in shifts),
    )(rank, bounds, q, do, delta, norm, opening, *kvs, *([] if first else [dq]))


def early_sum_body(*refs):
    total = refs[0][...]
    for part in refs[1:-1]:
        total = total + part[...].astype(F32)
    refs[-1][...] = total


def early_sum(own, parts):
    return pl.pallas_call(
        early_sum_body,
        out_shape=jax.ShapeDtypeStruct(own.shape, F32),
        compiler_params=vmem_params(),
        name="early_sum",
    )(own, *parts)


def share_body(early_ref, part_ref, out_ref):
    total = (early_ref[...] + part_ref[...].astype(F32)).astype(BF16)
    for n in range(out_ref.shape[0]):
        out_ref[n] = total


def share_copies(early, part, copies):
    return pl.pallas_call(
        share_body,
        out_shape=jax.ShapeDtypeStruct((copies,) + early.shape, BF16),
        compiler_params=vmem_params(),
        name="share_copies",
    )(early, part)


def product_body(core_ref, own_ref, other_ref, grad_ref, out_ref, acc_ref):
    step = pl.program_id(0)

    @pl.when(step == 0)
    def _():
        acc_ref[...] = jnp.zeros_like(acc_ref)

    grad = grad_ref[...].reshape(-1, grad_ref.shape[2])
    acc_ref[0] += dot(grad, own_ref[...].reshape(-1, own_ref.shape[2]), TN)
    acc_ref[1] += dot(grad, other_ref[...].reshape(-1, other_ref.shape[2]), TN)

    @pl.when(step == pl.num_programs(0) - 1)
    def _():
        low = acc_ref[core_ref[0]].astype(BF16)
        high = acc_ref[1 - core_ref[0]].astype(BF16)
        width = out_ref.shape[2]
        per_half = out_ref.shape[0] // 2
        for c in range(per_half):
            out_ref[c] = low[:, c * width : (c + 1) * width]
            out_ref[per_half + c] = high[:, c * width : (c + 1) * width]


def weight_product(core, own_half, other_half, grads, blocks):
    parts, rows, half = own_half.shape
    cols = grads.shape[2]
    width = 2 * half // blocks
    per_step = 2
    half_block = pl.BlockSpec((per_step, rows, half), lambda d: (d, 0, 0))
    return pl.pallas_call(
        product_body,
        grid=(parts // per_step,),
        in_specs=[
            pl.BlockSpec(memory_space=pltpu.SMEM),
            half_block,
            half_block,
            pl.BlockSpec((per_step, rows, cols), lambda d: (d, 0, 0)),
        ],
        out_specs=pl.BlockSpec((blocks, cols, width), lambda d: (0, 0, 0)),
        out_shape=jax.ShapeDtypeStruct((blocks, cols, width), BF16),
        scratch_shapes=[pltpu.VMEM((2, cols, half), F32)],
        compiler_params=vmem_params(),
        name="weight_product",
    )(core, own_half, other_half, grads)


def codes_body(parts_ref, dither_ref, out_ref):
    total = parts_ref[0].astype(F32)
    for n in range(1, parts_ref.shape[0]):
        total = total + parts_ref[n].astype(F32)
    for k in range(2):
        block = total[k * HEAD_SIZE : (k + 1) * HEAD_SIZE]
        largest = jnp.max(jnp.abs(block))
        scaled = 8.0 * block.T / (largest + 1e-06)
        out_ref[k] = scaled + (dither_ref[k].astype(F32) + 0.5) / 256.0


def weight_codes_of(parts, dither):
    return pl.pallas_call(
        codes_body,
        out_shape=jax.ShapeDtypeStruct(dither.shape, F32),
        compiler_params=vmem_params(),
        name="weight_codes",
    )(parts, dither)


def per_device(
    layer_input,
    queries,
    rotated_key_states,
    values,
    attention_out,
    output_grad,
    normalizer_shift,
    document_lengths,
    dither,
):
    context_size = lax.axis_size("context")
    dp_size = lax.axis_size("dp")
    rank = lax.axis_index("context").astype(jnp.int32).reshape(1)

    def send(x, by, sources=range(context_size)):
        return lax.ppermute(x, "context", [(i, (i + by) % context_size) for i in sources])

    def give_back(x, by):
        return send(x, -by, range(by, context_size))

    own_kv = jnp.concatenate([rotated_key_states[0], values[0]], axis=1)
    kv = {1: send(own_kv, 1), 6: send(own_kv, -2)}

    q, do = queries[0], output_grad[0]
    core = (lax.axis_index("tensor") % 2).astype(jnp.int32).reshape(1)
    delta, norm, opening, bounds, features = prepare(
        rank, core, document_lengths, normalizer_shift, attention_out[0], do, layer_input[0], dp_size
    )
    kv[1], kv[6], delta, features = lax.optimization_barrier((kv[1], kv[6], delta, features))
    own_half = lax.all_to_all(features, "dp", 0, 0)
    step = functools.partial(
        attention_step, rank=rank, bounds=bounds, q=q, do=do, delta=delta, norm=norm, opening=opening
    )
    back = []
    kv[2] = send(kv[1], 1)
    dq, term = step((1,), True, False, kvs=[kv[1]], dq=None)
    back.append(give_back(term, 1))
    kv[2], kv[6], dq = lax.optimization_barrier((kv[2], kv[6], dq))
    kv[3] = send(kv[2], 1)
    kv[5] = send(kv[6], -1)

    def work(shifts, dq):
        dq, *terms = step(shifts, False, False, kvs=[kv[s] for s in shifts], dq=dq)
        return dq, [give_back(term, s) for s, term in zip(shifts, terms, strict=True)]

    dq, terms = work((2, 6), dq)
    back += terms
    kv[3], kv[5], dq = lax.optimization_barrier((kv[3], kv[5], dq))
    kv[4] = send(kv[3], 1, range(3, context_size - 1))
    dq, middle = work((3, 5), dq)
    back += middle
    dq, (last,) = work((4,), dq)
    dq, own = step((0,), False, True, kvs=[own_kv], dq=dq)

    grads = share_copies(early_sum(own, back), last, dp_size)
    own_half, grads = lax.optimization_barrier((own_half, grads))
    swap = [(t, t ^ 1) for t in range(lax.axis_size("tensor"))]
    other_half = lax.ppermute(own_half, "tensor", swap)
    grads = lax.all_to_all(grads, "dp", 0, 0)
    product = weight_product(core, own_half, other_half, grads, context_size)
    parts = lax.all_to_all(product, "context", 0, 0)
    weight_codes = weight_codes_of(parts, dither)
    return (dq[None], weight_codes)


def solution(mesh):
    placed = (
        P("dp", "context", None),
        P("dp", "context", "tensor"),
        P("dp", "context", "tensor"),
        P("dp", "context", "tensor"),
        P("dp", "context", "tensor"),
        P("dp", "context", "tensor"),
        P("tensor"),
        P("dp", None),
        P(None, ("dp", "context"), "tensor"),
    )
    return jax.shard_map(
        per_device,
        mesh=mesh,
        in_specs=placed,
        out_specs=(P("dp", "context", "tensor"), P(None, ("dp", "context"), "tensor")),
        check_vma=False,
    )
```

profile of v0, /device:TPU:4, one launch (start us, length us, event | category | flops | bytes accessed | tf_op | source)
XLA Modules:
  0.0 158.7 jit_solution(12325699694909354504)
XLA Ops:
  0.6 1.0 pad_maximum_fusion.refs_7_
  1.6 6.4 %collective-permute-start.1 = (bf16[512,256]{1,0:T(8,128)(2,1)S(1)}, bf16[512,256]{1,0:T(8,128)(2,1)S(1)}, u32[]{:S(2)}, u32[]{:S(2)}) collective-permute-start(bf16[512,256]{1,0:T(8,128)(2,1)S(1)} %pad_maximum_fusion.refs_7_), channel_id=1, source_target_pairs={{0,24},{4,28},{8,0},{12,4},{16,8},{20,12},{24,16},{28,20},{1,25},{... | collective-permute-start | bytes 786440 | tf_op jit(solution)/shard_map/ppermute | solution.py:354
  8.0 1.0 collective-permute-start
  9.0 1.2 copy-done
  10.3 1.2 copy-done.4
  11.5 0.7 copy-done.6
  12.1 0.7 copy-done.7
  12.8 3.7 %prepare.1 = (f32[8,1,512]{2,1,0:T(1,128)S(1)}, f32[8,1,512]{2,1,0:T(1,128)S(1)}, s32[8,512]{1,0:T(8,128)S(1)}, s32[2]{0:T(128)S(1)}, bf16[8,512,512]{2,1,0:T(8,128)(2,1)S(1)}) custom-call(s32[1]{0:T(128)} %bitcast.rank_ref.refs_0_, s32[1]{0:T(128)} %bitcast.1.core_ref, s32[1,16]{1,0:T(1,128)S(1)} %copy-done.6, f32[8]{0:T(128)S(1)} %copy-done.7, ...), custom_call_target="tpu_custom_call" | custom-call | tf_op jit(solution)/shard_map/prepare/pallas_call | solution.py:87
  16.5 0.0 copy-start.3
  16.5 2.0 %copy-done.3 = bf16[8,512,512]{2,1,0:T(8,128)(2,1)} copy-done((bf16[8,512,512]{2,1,0:T(8,128)(2,1)}, bf16[8,512,512]{2,1,0:T(8,128)(2,1)S(1)}, u32[]{:S(2)}) %copy-start.3) | copy-done | bytes 4194328
  18.5 0.7 collective-permute-done.1.refs_8_
  19.2 0.0 collective-permute-done.refs_7_
  19.2 5.2 %all-to-all-start = ((bf16[8,512,512]{2,1,0:T(8,128)(2,1)}), bf16[8,512,512]{2,1,0:T(8,128)(2,1)}, u32[]{:S(2)}, u32[]{:S(2)}) async-start(bf16[8,512,512]{2,1,0:T(8,128)(2,1)} %copy-done.3), calls=%async_computation | async-start | bytes 8388608 | tf_op jit(solution)/shard_map/all_to_all | solution.py:368
  24.5 0.0 collective-permute-start.2
  24.5 0.0 copy-done.1
  24.5 1.1 attention_1.1
  25.6 7.4 %collective-permute-done.2.refs_7_ = bf16[512,256]{1,0:T(8,128)(2,1)S(1)} collective-permute-done((bf16[512,256]{1,0:T(8,128)(2,1)S(1)}, bf16[512,256]{1,0:T(8,128)(2,1)S(1)}, u32[]{:S(2)}, u32[]{:S(2)}) %collective-permute-start.2) | collective-permute-done | bytes 262176 | tf_op jit(solution)/shard_map/ppermute | solution.py:354
  33.0 1.4 collective-permute-start.3
  34.5 1.8 %collective-permute-start.4 = (bf16[512,256]{1,0:T(8,128)(2,1)S(1)}, bf16[512,256]{1,0:T(8,128)(2,1)S(1)}, u32[]{:S(2)}, u32[]{:S(2)}) collective-permute-start(bf16[512,256]{1,0:T(8,128)(2,1)S(1)} %collective-permute-done.1.refs_8_), channel_id=1, source_target_pairs={{0,28},{4,0},{8,4},{12,8},{16,12},{20,16},{24,20},{28,24},{1,29},{... | collective-permute-start | bytes 786440 | tf_op jit(solution)/shard_map/ppermute | solution.py:354
  36.3 1.3 attention_2_6.1
  37.6 3.3 %collective-permute-done.3.refs_7_ = bf16[512,256]{1,0:T(8,128)(2,1)S(1)} collective-permute-done((bf16[512,256]{1,0:T(8,128)(2,1)S(1)}, bf16[512,256]{1,0:T(8,128)(2,1)S(1)}, u32[]{:S(2)}, u32[]{:S(2)}) %collective-permute-start.3) | collective-permute-done | bytes 262176 | tf_op jit(solution)/shard_map/ppermute | solution.py:354
  40.8 0.3 collective-permute-done.4.refs_8_
  41.1 0.7 collective-permute-start.5
  41.8 1.3 collective-permute-start.6
  43.1 1.3 collective-permute-start.7
  44.4 1.3 collective-permute-start.8
  45.7 1.3 attention_3_5.1
  47.0 1.3 collective-permute-start.9
  48.3 0.0 collective-permute-done.5.refs_7_
  48.3 1.5 collective-permute-start.10
  49.8 1.1 attention_4.1
  51.0 0.5 collective-permute-done.6.refs_1_
  51.5 1.3 collective-permute-start.11
  52.8 7.8 %attention_0.1 = (bf16[512,1024]{1,0:T(8,128)(2,1)}, f32[512,256]{1,0:T(8,128)S(1)}) custom-call(s32[1]{0:T(128)} %bitcast.rank_ref.refs_0_, s32[2]{0:T(128)S(1)} %get-tuple-element.31.refs_1_, bf16[512,1024]{1,0:T(8,128)(2,1)S(1)} %bitcast.19, bf16[512,1024]{1,0:T(8,128)(2,1)S(1)} %bitcast.14, f32[8,1,512]{2,1,0:T(1,128)S(1)} %get-tuple-element.34.refs_4_, ...), custom_call_target="tpu_custom_call" | custom-call | flops 2097152 | bytes 1048576 | tf_op jit(solution)/shard_map/attention_0/pallas_call | solution.py:224
  60.6 0.0 collective-permute-done.7.refs_2_
  60.6 4.2 %collective-permute-done.8.refs_3_ = bf16[512,256]{1,0:T(8,128)(2,1)S(1)} collective-permute-done((bf16[512,256]{1,0:T(8,128)(2,1)S(1)}, bf16[512,256]{1,0:T(8,128)(2,1)S(1)}, u32[]{:S(2)}, u32[]{:S(2)}) %collective-permute-start.8) | collective-permute-done | bytes 262176 | tf_op jit(solution)/shard_map/ppermute | solution.py:354
  64.8 12.0 %collective-permute-done.9.refs_4_ = bf16[512,256]{1,0:T(8,128)(2,1)S(1)} collective-permute-done((bf16[512,256]{1,0:T(8,128)(2,1)S(1)}, bf16[512,256]{1,0:T(8,128)(2,1)S(1)}, u32[]{:S(2)}, u32[]{:S(2)}) %collective-permute-start.9) | collective-permute-done | bytes 262176 | tf_op jit(solution)/shard_map/ppermute | solution.py:354
  76.7 6.2 %collective-permute-done.10.refs_5_ = bf16[512,256]{1,0:T(8,128)(2,1)S(1)} collective-permute-done((bf16[512,256]{1,0:T(8,128)(2,1)S(1)}, bf16[512,256]{1,0:T(8,128)(2,1)S(1)}, u32[]{:S(2)}, u32[]{:S(2)}) %collective-permute-start.10) | collective-permute-done | bytes 262176 | tf_op jit(solution)/shard_map/ppermute | solution.py:354
  82.9 0.2 early_sum.1.early_ref
  83.1 0.0 collective-permute-done.11.part_ref
  83.1 0.1 share_copies.1
  83.2 0.0 all-to-all-done.own_ref
  83.2 0.1 collective-permute-start.12
  83.3 32.2 %all_to_all.15.grad_ref = bf16[8,512,256]{2,1,0:T(8,128)(2,1)S(1)} all-to-all(bf16[8,512,256]{2,1,0:T(8,128)(2,1)S(1)} %share_copies.1), channel_id=1, replica_groups=mesh['dp'=8,'context'=8,'tensor'=4] {'dp'}, dimensions={0} | all-to-all | bytes 4194304 | tf_op jit(solution)/shard_map/all_to_all | solution.py:397
  115.5 0.0 collective-permute-done.12.other_ref
  115.5 5.0 %weight_product.1 = bf16[8,256,128]{2,1,0:T(8,128)(2,1)S(1)} custom-call(s32[1]{0:T(128)} %bitcast.1.core_ref, bf16[8,512,512]{2,1,0:T(8,128)(2,1)} %all-to-all-done.own_ref, bf16[8,512,512]{2,1,0:T(8,128)(2,1)S(1)} %collective-permute-done.12.other_ref, bf16[8,512,256]{2,1,0:T(8,128)(2,1)S(1)} %all_to_all.15.grad_ref), custom_call_target="tpu_custom_call" | custom-call | tf_op jit(solution)/shard_map/weight_product/pallas_call | solution.py:301
  120.5 37.3 %all_to_all.16.parts_ref = bf16[8,256,128]{2,1,0:T(8,128)(2,1)S(1)} all-to-all(bf16[8,256,128]{2,1,0:T(8,128)(2,1)S(1)} %weight_product.1), channel_id=1, replica_groups=mesh['dp'=8,'context'=8,'tensor'=4] {'context'}, dimensions={0} | all-to-all | bytes 1048576 | tf_op jit(solution)/shard_map/all_to_all | solution.py:399
  157.8 0.9 weight_codes.1
  (9 shorter events, 0.0 us)
Async XLA Ops:
  1.6 17.6 %collective-permute-start.1 = (bf16[512,256]{1,0:T(8,128)(2,1)S(1)}, bf16[512,256]{1,0:T(8,128)(2,1)S(1)}, u32[]{:S(2)}, u32[]{:S(2)}) collective-permute-start(bf16[512,256]{1,0:T(8,128)(2,1)S(1)} %pad_maximum_fusion.refs_7_), channel_id=1, source_target_pairs={{0,24},{4,28},{8,0},{12,4},{16,8},{20,12},{24,16},{28,20},{1,25},{... | collective-permute-start | bytes 786440 | tf_op jit(solution)/shard_map/ppermute | solution.py:354
  8.0 11.2 %collective-permute-start = (bf16[512,256]{1,0:T(8,128)(2,1)S(1)}, bf16[512,256]{1,0:T(8,128)(2,1)S(1)}, u32[]{:S(2)}, u32[]{:S(2)}) collective-permute-start(bf16[512,256]{1,0:T(8,128)(2,1)S(1)} %pad_maximum_fusion.refs_7_), channel_id=1, source_target_pairs={{0,4},{4,8},{8,12},{12,16},{16,20},{20,24},{24,28},{28,0},{1,5},{5... | collective-permute-start | bytes 786440 | tf_op jit(solution)/shard_map/ppermute | solution.py:354
  9.0 1.2 copy-start
  10.3 1.2 copy-start.4
  11.5 0.7 copy-start.6
  12.1 0.7 copy-start.7
  16.5 2.0 %copy-start.3 = (bf16[8,512,512]{2,1,0:T(8,128)(2,1)}, bf16[8,512,512]{2,1,0:T(8,128)(2,1)S(1)}, u32[]{:S(2)}) copy-start(bf16[8,512,512]{2,1,0:T(8,128)(2,1)S(1)} %get-tuple-element.50) | copy-start | bytes 12582916
  19.2 5.3 %copy-start.1 = (bf16[1,512,1024]{2,1,0:T(8,128)(2,1)S(1)}, bf16[1,512,1024]{2,1,0:T(8,128)(2,1)}, u32[]{:S(2)}) copy-start(bf16[1,512,1024]{2,1,0:T(8,128)(2,1)} %param.14) | copy-start | bytes 3145732
  19.2 5.3 %copy-start.2 = (bf16[1,512,1024]{2,1,0:T(8,128)(2,1)S(1)}, bf16[1,512,1024]{2,1,0:T(8,128)(2,1)}, u32[]{:S(2)}) copy-start(bf16[1,512,1024]{2,1,0:T(8,128)(2,1)} %param.10) | copy-start | bytes 3145732
  19.2 64.0 %all-to-all-start = ((bf16[8,512,512]{2,1,0:T(8,128)(2,1)}), bf16[8,512,512]{2,1,0:T(8,128)(2,1)}, u32[]{:S(2)}, u32[]{:S(2)}) async-start(bf16[8,512,512]{2,1,0:T(8,128)(2,1)} %copy-done.3), calls=%async_computation | async-start | bytes 8388608 | tf_op jit(solution)/shard_map/all_to_all | solution.py:368
  24.5 8.6 %collective-permute-start.2 = (bf16[512,256]{1,0:T(8,128)(2,1)S(1)}, bf16[512,256]{1,0:T(8,128)(2,1)S(1)}, u32[]{:S(2)}, u32[]{:S(2)}) collective-permute-start(bf16[512,256]{1,0:T(8,128)(2,1)S(1)} %collective-permute-done.refs_7_), channel_id=1, source_target_pairs={{0,4},{4,8},{8,12},{12,16},{16,20},{20,24},{24,28},{28,0},{1,5},{5... | collective-permute-start | bytes 786440 | tf_op jit(solution)/shard_map/ppermute | solution.py:354
  33.0 7.8 %collective-permute-start.3 = (bf16[512,256]{1,0:T(8,128)(2,1)S(1)}, bf16[512,256]{1,0:T(8,128)(2,1)S(1)}, u32[]{:S(2)}, u32[]{:S(2)}) collective-permute-start(bf16[512,256]{1,0:T(8,128)(2,1)S(1)} %collective-permute-done.2.refs_7_), channel_id=1, source_target_pairs={{0,4},{4,8},{8,12},{12,16},{16,20},{20,24},{24,28},{28,0},{1,5},{5... | collective-permute-start | bytes 786440 | tf_op jit(solution)/shard_map/ppermute | solution.py:354
  34.5 6.7 %collective-permute-start.4 = (bf16[512,256]{1,0:T(8,128)(2,1)S(1)}, bf16[512,256]{1,0:T(8,128)(2,1)S(1)}, u32[]{:S(2)}, u32[]{:S(2)}) collective-permute-start(bf16[512,256]{1,0:T(8,128)(2,1)S(1)} %collective-permute-done.1.refs_8_), channel_id=1, source_target_pairs={{0,28},{4,0},{8,4},{12,8},{16,12},{20,16},{24,20},{28,24},{1,29},{... | collective-permute-start | bytes 786440 | tf_op jit(solution)/shard_map/ppermute | solution.py:354
  41.1 7.2 %collective-permute-start.5 = (bf16[512,256]{1,0:T(8,128)(2,1)S(1)}, bf16[512,256]{1,0:T(8,128)(2,1)S(1)}, u32[]{:S(2)}, u32[]{:S(2)}) collective-permute-start(bf16[512,256]{1,0:T(8,128)(2,1)S(1)} %collective-permute-done.3.refs_7_), channel_id=1, source_target_pairs={{12,16},{16,20},{20,24},{24,28},{13,17},{17,21},{21,25},{25,29},{1... | collective-permute-start | bytes 786440 | tf_op jit(solution)/shard_map/ppermute | solution.py:354
  41.8 9.7 %collective-permute-start.6 = (bf16[512,256]{1,0:T(8,128)(2,1)S(1)}, bf16[512,256]{1,0:T(8,128)(2,1)S(1)}, u32[]{:S(2)}, u32[]{:S(2)}) collective-permute-start(bf16[512,256]{1,0:T(8,128)(2,1)S(1)} %get-tuple-element.52), channel_id=1, source_target_pairs={{4,0},{8,4},{12,8},{16,12},{20,16},{24,20},{28,24},{5,1},{9,5},{13... | collective-permute-start | bytes 786440 | tf_op jit(solution)/shard_map/ppermute | solution.py:354
  43.1 17.4 %collective-permute-start.7 = (bf16[512,256]{1,0:T(8,128)(2,1)S(1)}, bf16[512,256]{1,0:T(8,128)(2,1)S(1)}, u32[]{:S(2)}, u32[]{:S(2)}) collective-permute-start(bf16[512,256]{1,0:T(8,128)(2,1)S(1)} %get-tuple-element.53), channel_id=1, source_target_pairs={{8,0},{12,4},{16,8},{20,12},{24,16},{28,20},{9,1},{13,5},{17,9},{2... | collective-permute-start | bytes 786440 | tf_op jit(solution)/shard_map/ppermute | solution.py:354
  44.4 20.3 %collective-permute-start.8 = (bf16[512,256]{1,0:T(8,128)(2,1)S(1)}, bf16[512,256]{1,0:T(8,128)(2,1)S(1)}, u32[]{:S(2)}, u32[]{:S(2)}) collective-permute-start(bf16[512,256]{1,0:T(8,128)(2,1)S(1)} %get-tuple-element.54), channel_id=1, source_target_pairs={{24,0},{28,4},{25,1},{29,5},{26,2},{30,6},{27,3},{31,7},{56,32},{6... | collective-permute-start | bytes 786440 | tf_op jit(solution)/shard_map/ppermute | solution.py:354
  47.0 29.7 %collective-permute-start.9 = (bf16[512,256]{1,0:T(8,128)(2,1)S(1)}, bf16[512,256]{1,0:T(8,128)(2,1)S(1)}, u32[]{:S(2)}, u32[]{:S(2)}) collective-permute-start(bf16[512,256]{1,0:T(8,128)(2,1)S(1)} %get-tuple-element.55), channel_id=1, source_target_pairs={{12,0},{16,4},{20,8},{24,12},{28,16},{13,1},{17,5},{21,9},{25,13},... | collective-permute-start | bytes 786440 | tf_op jit(solution)/shard_map/ppermute | solution.py:354
  48.3 34.6 %collective-permute-start.10 = (bf16[512,256]{1,0:T(8,128)(2,1)S(1)}, bf16[512,256]{1,0:T(8,128)(2,1)S(1)}, u32[]{:S(2)}, u32[]{:S(2)}) collective-permute-start(bf16[512,256]{1,0:T(8,128)(2,1)S(1)} %get-tuple-element.56), channel_id=1, source_target_pairs={{20,0},{24,4},{28,8},{21,1},{25,5},{29,9},{22,2},{26,6},{30,10},{2... | collective-permute-start | bytes 786440 | tf_op jit(solution)/shard_map/ppermute | solution.py:354
  51.5 31.6 %collective-permute-start.11 = (bf16[512,256]{1,0:T(8,128)(2,1)S(1)}, bf16[512,256]{1,0:T(8,128)(2,1)S(1)}, u32[]{:S(2)}, u32[]{:S(2)}) collective-permute-start(bf16[512,256]{1,0:T(8,128)(2,1)S(1)} %get-tuple-element.57), channel_id=1, source_target_pairs={{16,0},{20,4},{24,8},{28,12},{17,1},{21,5},{25,9},{29,13},{18,2},{... | collective-permute-start | bytes 786440 | tf_op jit(solution)/shard_map/ppermute | solution.py:354
  83.2 32.3 %collective-permute-start.12 = (bf16[8,512,512]{2,1,0:T(8,128)(2,1)}, bf16[8,512,512]{2,1,0:T(8,128)(2,1)S(1)}, u32[]{:S(2)}, u32[]{:S(2)}) collective-permute-start(bf16[8,512,512]{2,1,0:T(8,128)(2,1)} %all-to-all-done.own_ref), channel_id=1, source_target_pairs={{0,1},{1,0},{2,3},{3,2},{4,5},{5,4},{6,7},{7,6},{8,9},{9,8},{10,11... | collective-permute-start | bytes 12582920 | tf_op jit(solution)/shard_map/ppermute | solution.py:396
  115.5 42.3 %copy-start.5 = (s32[2,128,128]{2,1,0:T(8,128)S(1)}, s32[2,128,128]{2,1,0:T(8,128)}, u32[]{:S(2)}) copy-start(s32[2,128,128]{2,1,0:T(8,128)} %dither_ref.1) | copy-start | bytes 393220
where the time goes:
time: 159 us
  blocking collectives  69.5 us (44%)
  waiting for transfers between devices  34.6 us (22%)
  starting transfers between devices  24.6 us (15%)
  Pallas kernels  22.4 us (14%)
  local copies, waits for them, and re-layouts  5.79 us (4%)
    all_to_all x1, blocking collectives, per_device(): parts = lax.all_to_all(product, 'context', 0, 0)  37.3 us
    ppermute x12, waiting for transfers between devices, send(): lax.ppermute(x, 'context', [(i, (i + by) % context_size) for i in sources])  34.6 us
    all_to_all x1, blocking collectives, per_device(): grads = lax.all_to_all(grads, 'dp', 0, 0)  32.2 us
    ppermute x12, starting transfers between devices, send(): lax.ppermute(x, 'context', [(i, (i + by) % context_size) for i in sources])  19.3 us
    pallas_call x5, Pallas kernels, attention_step(): pl.pallas_call(functools.partial(attention_body, shifts, first, last), gr...  12.6 us
    unnamed x16, local copies, waits for them, and re-layouts  5.79 us
    all_to_all x1, starting transfers between devices, per_device(): own_half = lax.all_to_all(features, 'dp', 0, 0)  5.24 us
    pallas_call x1, Pallas kernels, weight_product(): pl.pallas_call(product_body, grid=(parts // per_step,), in_specs=[pl.Bloc...  5 us
  transfers between devices with their start and end apart: 14, of which 8 were waited for; matrix products, arithmetic and copies ran while one was open for 0% of the time, Pallas kernels for 10%

commit v1 on v0

--- a/solution.py
+++ b/solution.py
@@ -175,8 +175,9 @@
 
     if shifts == (0,):
         masked_block(0, start, True)
-    elif blocks == 1:
-        block(0, shifts[0])
+    elif min(shifts) > 2 or blocks == 1:
+        for b in range(blocks):
+            block(b, shifts[b])
     else:
 
         def each(b, _):

time: 159 us -> 160 us (level)
  transfers between devices with their start and end apart: 14 -> 14, of which waited for: 8 -> 7; matrix products, arithmetic and copies ran while one was open for 0% -> 0% of each run, Pallas kernels for 10% -> 10%
where the time goes in v1:
time: 160 us; the launch traced here: 159 us
  blocking collectives  70.7 us (44%)
  waiting for transfers between devices  34 us (21%)
  starting transfers between devices  24.6 us (15%)
  Pallas kernels  22.4 us (14%)
  local copies, waits for them, and re-layouts  5.79 us (4%)
    all_to_all x1, blocking collectives, per_device(): parts = lax.all_to_all(product, 'context', 0, 0)  37.7 us
    ppermute x12, waiting for transfers between devices, send(): lax.ppermute(x, 'context', [(i, (i + by) % context_size) for i in sources])  34 us
    all_to_all x1, blocking collectives, per_device(): grads = lax.all_to_all(grads, 'dp', 0, 0)  32.9 us
    ppermute x12, starting transfers between devices, send(): lax.ppermute(x, 'context', [(i, (i + by) % context_size) for i in sources])  19.3 us
    pallas_call x5, Pallas kernels, attention_step(): pl.pallas_call(functools.partial(attention_body, shifts, first, last), gr...  12.5 us
    unnamed x16, local copies, waits for them, and re-layouts  5.79 us
    all_to_all x1, starting transfers between devices, per_device(): own_half = lax.all_to_all(features, 'dp', 0, 0)  5.24 us
    pallas_call x1, Pallas kernels, weight_product(): pl.pallas_call(product_body, grid=(parts // per_step,), in_specs=[pl.Bloc...  5.01 us
  transfers between devices with their start and end apart: 14, of which 7 were waited for; matrix products, arithmetic and copies ran while one was open for 0% of the time, Pallas kernels for 10%

profile of v1, /device:TPU:4, one launch (start us, length us, event | category | flops | bytes accessed | tf_op | source)
XLA Modules:
  0.0 159.3 jit_solution(7154098560984794035)
XLA Ops:
  0.6 1.0 pad_maximum_fusion.refs_7_
  1.6 6.4 %collective-permute-start.1 = (bf16[512,256]{1,0:T(8,128)(2,1)S(1)}, bf16[512,256]{1,0:T(8,128)(2,1)S(1)}, u32[]{:S(2)}, u32[]{:S(2)}) collective-permute-start(bf16[512,256]{1,0:T(8,128)(2,1)S(1)} %pad_maximum_fusion.refs_7_), channel_id=1, source_target_pairs={{0,24},{4,28},{8,0},{12,4},{16,8},{20,12},{24,16},{28,20},{1,25},{... | collective-permute-start | bytes 786440 | tf_op jit(solution)/shard_map/ppermute | solution.py:355
  8.0 1.0 collective-permute-start
  9.0 1.2 copy-done
  10.3 1.2 copy-done.4
  11.5 0.7 copy-done.6
  12.1 0.7 copy-done.7
  12.8 3.7 %prepare.1 = (f32[8,1,512]{2,1,0:T(1,128)S(1)}, f32[8,1,512]{2,1,0:T(1,128)S(1)}, s32[8,512]{1,0:T(8,128)S(1)}, s32[2]{0:T(128)S(1)}, bf16[8,512,512]{2,1,0:T(8,128)(2,1)S(1)}) custom-call(s32[1]{0:T(128)} %bitcast.rank_ref.refs_0_, s32[1]{0:T(128)} %bitcast.1.core_ref, s32[1,16]{1,0:T(1,128)S(1)} %copy-done.6, f32[8]{0:T(128)S(1)} %copy-done.7, ...), custom_call_target="tpu_custom_call" | custom-call | tf_op jit(solution)/shard_map/prepare/pallas_call | solution.py:87
  16.5 0.0 copy-start.3
  16.5 2.0 %copy-done.3 = bf16[8,512,512]{2,1,0:T(8,128)(2,1)} copy-done((bf16[8,512,512]{2,1,0:T(8,128)(2,1)}, bf16[8,512,512]{2,1,0:T(8,128)(2,1)S(1)}, u32[]{:S(2)}) %copy-start.3) | copy-done | bytes 4194328
  18.5 0.7 collective-permute-done.1.refs_8_
  19.2 0.0 collective-permute-done.refs_7_
  19.2 5.2 %all-to-all-start = ((bf16[8,512,512]{2,1,0:T(8,128)(2,1)}), bf16[8,512,512]{2,1,0:T(8,128)(2,1)}, u32[]{:S(2)}, u32[]{:S(2)}) async-start(bf16[8,512,512]{2,1,0:T(8,128)(2,1)} %copy-done.3), calls=%async_computation | async-start | bytes 8388608 | tf_op jit(solution)/shard_map/all_to_all | solution.py:369
  24.5 0.0 collective-permute-start.2
  24.5 0.0 copy-done.1
  24.5 1.1 attention_1.1
  25.6 7.4 %collective-permute-done.2.refs_7_ = bf16[512,256]{1,0:T(8,128)(2,1)S(1)} collective-permute-done((bf16[512,256]{1,0:T(8,128)(2,1)S(1)}, bf16[512,256]{1,0:T(8,128)(2,1)S(1)}, u32[]{:S(2)}, u32[]{:S(2)}) %collective-permute-start.2) | collective-permute-done | bytes 262176 | tf_op jit(solution)/shard_map/ppermute | solution.py:355
  33.0 1.4 collective-permute-start.3
  34.5 1.8 %collective-permute-start.4 = (bf16[512,256]{1,0:T(8,128)(2,1)S(1)}, bf16[512,256]{1,0:T(8,128)(2,1)S(1)}, u32[]{:S(2)}, u32[]{:S(2)}) collective-permute-start(bf16[512,256]{1,0:T(8,128)(2,1)S(1)} %collective-permute-done.1.refs_8_), channel_id=1, source_target_pairs={{0,28},{4,0},{8,4},{12,8},{16,12},{20,16},{24,20},{28,24},{1,29},{... | collective-permute-start | bytes 786440 | tf_op jit(solution)/shard_map/ppermute | solution.py:355
  36.3 1.3 attention_2_6.1
  37.6 3.3 %collective-permute-done.3.refs_7_ = bf16[512,256]{1,0:T(8,128)(2,1)S(1)} collective-permute-done((bf16[512,256]{1,0:T(8,128)(2,1)S(1)}, bf16[512,256]{1,0:T(8,128)(2,1)S(1)}, u32[]{:S(2)}, u32[]{:S(2)}) %collective-permute-start.3) | collective-permute-done | bytes 262176 | tf_op jit(solution)/shard_map/ppermute | solution.py:355
  40.8 0.3 collective-permute-done.4.refs_8_
  41.1 0.7 collective-permute-start.5
  41.8 1.3 collective-permute-start.6
  43.1 1.3 collective-permute-start.7
  44.4 1.3 collective-permute-start.8
  45.7 1.2 attention_3_5.1
  47.0 1.3 collective-permute-start.9
  48.3 0.0 collective-permute-done.5.refs_7_
  48.3 1.5 collective-permute-start.10
  49.8 1.1 attention_4.1
  50.9 1.3 collective-permute-done.6.refs_1_
  52.2 1.3 collective-permute-start.11
  53.5 7.8 %attention_0.1 = (bf16[512,1024]{1,0:T(8,128)(2,1)}, f32[512,256]{1,0:T(8,128)S(1)}) custom-call(s32[1]{0:T(128)} %bitcast.rank_ref.refs_0_, s32[2]{0:T(128)S(1)} %get-tuple-element.31.refs_1_, bf16[512,1024]{1,0:T(8,128)(2,1)S(1)} %bitcast.19, bf16[512,1024]{1,0:T(8,128)(2,1)S(1)} %bitcast.14, f32[8,1,512]{2,1,0:T(1,128)S(1)} %get-tuple-element.34.refs_4_, ...), custom_call_target="tpu_custom_call" | custom-call | flops 2097152 | bytes 1048576 | tf_op jit(solution)/shard_map/attention_0/pallas_call | solution.py:225
  61.3 0.0 collective-permute-done.7.refs_2_
  61.3 11.1 %collective-permute-done.8.refs_3_ = bf16[512,256]{1,0:T(8,128)(2,1)S(1)} collective-permute-done((bf16[512,256]{1,0:T(8,128)(2,1)S(1)}, bf16[512,256]{1,0:T(8,128)(2,1)S(1)}, u32[]{:S(2)}, u32[]{:S(2)}) %collective-permute-start.8) | collective-permute-done | bytes 262176 | tf_op jit(solution)/shard_map/ppermute | solution.py:355
  72.4 9.9 %collective-permute-done.9.refs_4_ = bf16[512,256]{1,0:T(8,128)(2,1)S(1)} collective-permute-done((bf16[512,256]{1,0:T(8,128)(2,1)S(1)}, bf16[512,256]{1,0:T(8,128)(2,1)S(1)}, u32[]{:S(2)}, u32[]{:S(2)}) %collective-permute-start.9) | collective-permute-done | bytes 262176 | tf_op jit(solution)/shard_map/ppermute | solution.py:355
  82.3 0.0 collective-permute-done.10.refs_5_
  82.3 0.2 early_sum.1.early_ref
  82.5 0.0 collective-permute-done.11.part_ref
  82.5 0.1 share_copies.1
  82.6 0.0 all-to-all-done.own_ref
  82.6 0.1 collective-permute-start.12
  82.7 32.9 %all_to_all.15.grad_ref = bf16[8,512,256]{2,1,0:T(8,128)(2,1)S(1)} all-to-all(bf16[8,512,256]{2,1,0:T(8,128)(2,1)S(1)} %share_copies.1), channel_id=1, replica_groups=mesh['dp'=8,'context'=8,'tensor'=4] {'dp'}, dimensions={0} | all-to-all | bytes 4194304 | tf_op jit(solution)/shard_map/all_to_all | solution.py:398
  115.7 0.0 collective-permute-done.12.other_ref
  115.7 5.0 %weight_product.1 = bf16[8,256,128]{2,1,0:T(8,128)(2,1)S(1)} custom-call(s32[1]{0:T(128)} %bitcast.1.core_ref, bf16[8,512,512]{2,1,0:T(8,128)(2,1)} %all-to-all-done.own_ref, bf16[8,512,512]{2,1,0:T(8,128)(2,1)S(1)} %collective-permute-done.12.other_ref, bf16[8,512,256]{2,1,0:T(8,128)(2,1)S(1)} %all_to_all.15.grad_ref), custom_call_target="tpu_custom_call" | custom-call | tf_op jit(solution)/shard_map/weight_product/pallas_call | solution.py:302
  120.7 37.7 %all_to_all.16.parts_ref = bf16[8,256,128]{2,1,0:T(8,128)(2,1)S(1)} all-to-all(bf16[8,256,128]{2,1,0:T(8,128)(2,1)S(1)} %weight_product.1), channel_id=1, replica_groups=mesh['dp'=8,'context'=8,'tensor'=4] {'context'}, dimensions={0} | all-to-all | bytes 1048576 | tf_op jit(solution)/shard_map/all_to_all | solution.py:400
  158.4 0.9 weight_codes.1
  (9 shorter events, 0.0 us)
Async XLA Ops:
  1.6 17.6 %collective-permute-start.1 = (bf16[512,256]{1,0:T(8,128)(2,1)S(1)}, bf16[512,256]{1,0:T(8,128)(2,1)S(1)}, u32[]{:S(2)}, u32[]{:S(2)}) collective-permute-start(bf16[512,256]{1,0:T(8,128)(2,1)S(1)} %pad_maximum_fusion.refs_7_), channel_id=1, source_target_pairs={{0,24},{4,28},{8,0},{12,4},{16,8},{20,12},{24,16},{28,20},{1,25},{... | collective-permute-start | bytes 786440 | tf_op jit(solution)/shard_map/ppermute | solution.py:355
  8.0 11.2 %collective-permute-start = (bf16[512,256]{1,0:T(8,128)(2,1)S(1)}, bf16[512,256]{1,0:T(8,128)(2,1)S(1)}, u32[]{:S(2)}, u32[]{:S(2)}) collective-permute-start(bf16[512,256]{1,0:T(8,128)(2,1)S(1)} %pad_maximum_fusion.refs_7_), channel_id=1, source_target_pairs={{0,4},{4,8},{8,12},{12,16},{16,20},{20,24},{24,28},{28,0},{1,5},{5... | collective-permute-start | bytes 786440 | tf_op jit(solution)/shard_map/ppermute | solution.py:355
  9.0 1.2 copy-start
  10.3 1.2 copy-start.4
  11.5 0.7 copy-start.6
  12.1 0.7 copy-start.7
  16.5 2.0 %copy-start.3 = (bf16[8,512,512]{2,1,0:T(8,128)(2,1)}, bf16[8,512,512]{2,1,0:T(8,128)(2,1)S(1)}, u32[]{:S(2)}) copy-start(bf16[8,512,512]{2,1,0:T(8,128)(2,1)S(1)} %get-tuple-element.50) | copy-start | bytes 12582916
  19.2 5.3 %copy-start.1 = (bf16[1,512,1024]{2,1,0:T(8,128)(2,1)S(1)}, bf16[1,512,1024]{2,1,0:T(8,128)(2,1)}, u32[]{:S(2)}) copy-start(bf16[1,512,1024]{2,1,0:T(8,128)(2,1)} %param.14) | copy-start | bytes 3145732
  19.2 5.3 %copy-start.2 = (bf16[1,512,1024]{2,1,0:T(8,128)(2,1)S(1)}, bf16[1,512,1024]{2,1,0:T(8,128)(2,1)}, u32[]{:S(2)}) copy-start(bf16[1,512,1024]{2,1,0:T(8,128)(2,1)} %param.10) | copy-start | bytes 3145732
  19.2 63.4 %all-to-all-start = ((bf16[8,512,512]{2,1,0:T(8,128)(2,1)}), bf16[8,512,512]{2,1,0:T(8,128)(2,1)}, u32[]{:S(2)}, u32[]{:S(2)}) async-start(bf16[8,512,512]{2,1,0:T(8,128)(2,1)} %copy-done.3), calls=%async_computation | async-start | bytes 8388608 | tf_op jit(solution)/shard_map/all_to_all | solution.py:369
  24.5 8.6 %collective-permute-start.2 = (bf16[512,256]{1,0:T(8,128)(2,1)S(1)}, bf16[512,256]{1,0:T(8,128)(2,1)S(1)}, u32[]{:S(2)}, u32[]{:S(2)}) collective-permute-start(bf16[512,256]{1,0:T(8,128)(2,1)S(1)} %collective-permute-done.refs_7_), channel_id=1, source_target_pairs={{0,4},{4,8},{8,12},{12,16},{16,20},{20,24},{24,28},{28,0},{1,5},{5... | collective-permute-start | bytes 786440 | tf_op jit(solution)/shard_map/ppermute | solution.py:355
  33.0 7.8 %collective-permute-start.3 = (bf16[512,256]{1,0:T(8,128)(2,1)S(1)}, bf16[512,256]{1,0:T(8,128)(2,1)S(1)}, u32[]{:S(2)}, u32[]{:S(2)}) collective-permute-start(bf16[512,256]{1,0:T(8,128)(2,1)S(1)} %collective-permute-done.2.refs_7_), channel_id=1, source_target_pairs={{0,4},{4,8},{8,12},{12,16},{16,20},{20,24},{24,28},{28,0},{1,5},{5... | collective-permute-start | bytes 786440 | tf_op jit(solution)/shard_map/ppermute | solution.py:355
  34.5 6.7 %collective-permute-start.4 = (bf16[512,256]{1,0:T(8,128)(2,1)S(1)}, bf16[512,256]{1,0:T(8,128)(2,1)S(1)}, u32[]{:S(2)}, u32[]{:S(2)}) collective-permute-start(bf16[512,256]{1,0:T(8,128)(2,1)S(1)} %collective-permute-done.1.refs_8_), channel_id=1, source_target_pairs={{0,28},{4,0},{8,4},{12,8},{16,12},{20,16},{24,20},{28,24},{1,29},{... | collective-permute-start | bytes 786440 | tf_op jit(solution)/shard_map/ppermute | solution.py:355
  41.1 7.1 %collective-permute-start.5 = (bf16[512,256]{1,0:T(8,128)(2,1)S(1)}, bf16[512,256]{1,0:T(8,128)(2,1)S(1)}, u32[]{:S(2)}, u32[]{:S(2)}) collective-permute-start(bf16[512,256]{1,0:T(8,128)(2,1)S(1)} %collective-permute-done.3.refs_7_), channel_id=1, source_target_pairs={{12,16},{16,20},{20,24},{24,28},{13,17},{17,21},{21,25},{25,29},{1... | collective-permute-start | bytes 786440 | tf_op jit(solution)/shard_map/ppermute | solution.py:355
  41.8 10.4 %collective-permute-start.6 = (bf16[512,256]{1,0:T(8,128)(2,1)S(1)}, bf16[512,256]{1,0:T(8,128)(2,1)S(1)}, u32[]{:S(2)}, u32[]{:S(2)}) collective-permute-start(bf16[512,256]{1,0:T(8,128)(2,1)S(1)} %get-tuple-element.52), channel_id=1, source_target_pairs={{4,0},{8,4},{12,8},{16,12},{20,16},{24,20},{28,24},{5,1},{9,5},{13... | collective-permute-start | bytes 786440 | tf_op jit(solution)/shard_map/ppermute | solution.py:355
  43.1 18.2 %collective-permute-start.7 = (bf16[512,256]{1,0:T(8,128)(2,1)S(1)}, bf16[512,256]{1,0:T(8,128)(2,1)S(1)}, u32[]{:S(2)}, u32[]{:S(2)}) collective-permute-start(bf16[512,256]{1,0:T(8,128)(2,1)S(1)} %get-tuple-element.53), channel_id=1, source_target_pairs={{8,0},{12,4},{16,8},{20,12},{24,16},{28,20},{9,1},{13,5},{17,9},{2... | collective-permute-start | bytes 786440 | tf_op jit(solution)/shard_map/ppermute | solution.py:355
  44.4 28.0 %collective-permute-start.8 = (bf16[512,256]{1,0:T(8,128)(2,1)S(1)}, bf16[512,256]{1,0:T(8,128)(2,1)S(1)}, u32[]{:S(2)}, u32[]{:S(2)}) collective-permute-start(bf16[512,256]{1,0:T(8,128)(2,1)S(1)} %get-tuple-element.54), channel_id=1, source_target_pairs={{24,0},{28,4},{25,1},{29,5},{26,2},{30,6},{27,3},{31,7},{56,32},{6... | collective-permute-start | bytes 786440 | tf_op jit(solution)/shard_map/ppermute | solution.py:355
  47.0 35.3 %collective-permute-start.9 = (bf16[512,256]{1,0:T(8,128)(2,1)S(1)}, bf16[512,256]{1,0:T(8,128)(2,1)S(1)}, u32[]{:S(2)}, u32[]{:S(2)}) collective-permute-start(bf16[512,256]{1,0:T(8,128)(2,1)S(1)} %get-tuple-element.55), channel_id=1, source_target_pairs={{12,0},{16,4},{20,8},{24,12},{28,16},{13,1},{17,5},{21,9},{25,13},... | collective-permute-start | bytes 786440 | tf_op jit(solution)/shard_map/ppermute | solution.py:355
  48.3 34.0 %collective-permute-start.10 = (bf16[512,256]{1,0:T(8,128)(2,1)S(1)}, bf16[512,256]{1,0:T(8,128)(2,1)S(1)}, u32[]{:S(2)}, u32[]{:S(2)}) collective-permute-start(bf16[512,256]{1,0:T(8,128)(2,1)S(1)} %get-tuple-element.56), channel_id=1, source_target_pairs={{20,0},{24,4},{28,8},{21,1},{25,5},{29,9},{22,2},{26,6},{30,10},{2... | collective-permute-start | bytes 786440 | tf_op jit(solution)/shard_map/ppermute | solution.py:355
  52.2 30.3 %collective-permute-start.11 = (bf16[512,256]{1,0:T(8,128)(2,1)S(1)}, bf16[512,256]{1,0:T(8,128)(2,1)S(1)}, u32[]{:S(2)}, u32[]{:S(2)}) collective-permute-start(bf16[512,256]{1,0:T(8,128)(2,1)S(1)} %get-tuple-element.57), channel_id=1, source_target_pairs={{16,0},{20,4},{24,8},{28,12},{17,1},{21,5},{25,9},{29,13},{18,2},{... | collective-permute-start | bytes 786440 | tf_op jit(solution)/shard_map/ppermute | solution.py:355
  82.6 33.0 %collective-permute-start.12 = (bf16[8,512,512]{2,1,0:T(8,128)(2,1)}, bf16[8,512,512]{2,1,0:T(8,128)(2,1)S(1)}, u32[]{:S(2)}, u32[]{:S(2)}) collective-permute-start(bf16[8,512,512]{2,1,0:T(8,128)(2,1)} %all-to-all-done.own_ref), channel_id=1, source_target_pairs={{0,1},{1,0},{2,3},{3,2},{4,5},{5,4},{6,7},{7,6},{8,9},{9,8},{10,11... | collective-permute-start | bytes 12582920 | tf_op jit(solution)/shard_map/ppermute | solution.py:397
  115.7 42.8 %copy-start.5 = (s32[2,128,128]{2,1,0:T(8,128)S(1)}, s32[2,128,128]{2,1,0:T(8,128)}, u32[]{:S(2)}) copy-start(s32[2,128,128]{2,1,0:T(8,128)} %dither_ref.1) | copy-start | bytes 393220
